TPU v7x, 32 devices: a whole 2x2x4 slice. The times are simulated.
32 devices in a mesh: tok: 8 (over z, core), cell: 4 (over y, x).
Axes of the slice: x: 2, y: 2, z: 4, core: 2. Of those that a mesh axis runs over, the one named last changes fastest.
Arguments:
- activations: bfloat16 [8192, 4096], P('tok'), may hold values from -6 to 6
- out_grads: bfloat16 [8192, 1024], P('tok'), may hold values from -6 to 6
- query_ids: int32 [8192], P('tok'), may hold values from 0 to 511
- live: int32 [8], P('tok'), may hold values from 256 to 1024, as said below
- proj_in: bfloat16 [4096, 64], P(None, 'cell'), may hold values from -0.09375 to 0.09375
- proj_out: bfloat16 [1024, 32], replicated, may hold values from -0.1875 to 0.1875
- whitener: bfloat16 [2048, 2048], P('cell')
- stores: bfloat16 [49152, 2048], P(('tok', 'cell')), may hold values from -0.023925781 to 0.023925781
Outputs:
- scores: float32 [512, 49152], P(None, ('tok', 'cell'))
Inputs may be any that keep to these rules, and one draw needn't show every extreme that they name: `live`: each entry is a count of valid tokens of one block of 1024; some block is full in every draw.
All inputs are finite; a program needn't handle non-finite values.
Results may differ from a plain program's by a relative error of at most 0.005.
Values may be sent and summed in bfloat16 or wider, within the bound.
A program may use at most 64 MiB of HBM per device.

v0:
```python
import functools

import jax
import jax.numpy as jnp
from jax import lax
from jax.experimental import pallas as pl
from jax.experimental.pallas import tpu as pltpu
from jax.sharding import PartitionSpec as P

Q = 512
CORES = 2
MESH = pl.DeviceIdType.MESH
F32 = jnp.float32
BF16 = jnp.bfloat16


def tile_of(extent, most):
    size = min(extent, most)
    while extent % size:
        size //= 2
    return size


def dot(a, b):
    return jnp.dot(a, b, preferred_element_type=F32)


def dot_t(a, b):
    return lax.dot_general(a, b, (((1,), (1,)), ((), ())), preferred_element_type=F32)


def spread(values, pattern):
    high = values.astype(BF16)
    low = (values - high.astype(F32)).astype(BF16)
    return dot(high, pattern) + dot(low, pattern)


def kernel(
    nt, nc, act_hbm, og_hbm, ids_hbm, live_ref, pin_hbm, pout_hbm, wh_hbm, st_hbm, out_ref,
    act, og, ids_ref, pin, pout, wh, st, outer, hot, sib_out, sib_in, own, z_out, z_in, summed, c_out, c_in, own_w, gath,
    load_sem, sib_sem, z_sem, c_sem, gz_sem, gc_sem, gs_sem,
):
    tok = lax.axis_index("tok")
    cell = lax.axis_index("cell")
    nz = nt // CORES
    zz = tok // CORES
    core = tok % CORES
    toks, fc = outer.shape
    qb = Q // nt
    fw = wh.shape[2]
    ra, rb = pin.shape[0], pout.shape[0]
    bits = nc.bit_length() - 1

    def cell_at(m):
        other = cell
        for k in range(bits):
            if m & (1 << k):
                other = other + (1 << k) * (1 - 2 * ((cell // (1 << k)) % 2))
        return other

    def z_at(j):
        return ((zz + j) % nz) * CORES + core

    def z_from(j):
        return ((zz + nz - j) % nz) * CORES

    sibling = zz * CORES + (1 - core)

    barrier = pltpu.get_barrier_semaphore()
    pl.semaphore_signal(barrier, inc=1, device_id={"tok": sibling}, device_id_type=MESH)
    for j in range(1, nz):
        pl.semaphore_signal(barrier, inc=1, device_id={"tok": z_at(j)}, device_id_type=MESH)
    for m in range(1, nc):
        pl.semaphore_signal(barrier, inc=1, device_id={"cell": cell_at(m)}, device_id_type=MESH)

    rows = tile_of(toks, 256)
    steps = toks // rows
    loads = []

    def load(src, dst):
        copy = pltpu.make_async_copy(src, dst, load_sem.at[len(loads)])
        copy.start()
        loads.append(copy)
        return copy

    ids_load = load(ids_hbm, ids_ref)
    pin_load = load(pin_hbm, pin)
    pout_load = load(pout_hbm, pout)
    chunk_loads = []
    for s in range(steps):
        part = pl.ds(s * rows, rows)
        chunk_loads.append((load(og_hbm.at[part], og.at[part]), load(act_hbm.at[part], act.at[part])))
    wh_loads, st_loads = [], []
    for m in range(nc):
        cols = pl.ds(pl.multiple_of(cell_at(m) * fw, fw), fw)
        wh_loads.append(load(wh_hbm.at[:, cols], wh.at[m]))

    ids_load.wait()
    ids = ids_ref[...]
    valid = lax.broadcasted_iota(jnp.int32, (1, toks), 1) < live_ref[0]
    ids = jnp.where(valid, ids, -1)
    row = lax.broadcasted_iota(jnp.int32, (qb, toks), 0)
    for side in range(2):
        parity = 1 - core if side == 0 else core
        for j in range(nz):
            first = (((zz + j) % nz) * CORES + parity) * qb
            hot[side, pl.ds(j * qb, qb), :] = (row + first == ids).astype(F32).astype(BF16)

    feat = lax.broadcasted_iota(jnp.int32, (ra, fc), 1)
    at = lax.broadcasted_iota(jnp.int32, (ra, fc), 0)
    left_pat = ((feat >= at * rb) & (feat < at * rb + rb)).astype(F32).astype(BF16)
    feat = lax.broadcasted_iota(jnp.int32, (rb, fc), 1)
    at = lax.broadcasted_iota(jnp.int32, (rb, fc), 0)
    right_pat = (jnp.bitwise_and(feat, rb - 1) == at).astype(F32).astype(BF16)

    pin_load.wait()
    pout_load.wait()
    for s in range(steps):
        part = pl.ds(s * rows, rows)
        chunk_loads[s][0].wait()
        right = dot_t(og[part, :], pout[...])
        chunk_loads[s][1].wait()
        left = dot_t(act[part, :], pin[...])
        outer[part, :] = (spread(left, left_pat) * spread(right, right_pat)).astype(BF16)

    for m in range(nc):
        cols = pl.ds(pl.multiple_of(cell_at(m) * fw, fw), fw)
        st_loads.append(load(st_hbm.at[:, cols], st.at[m]))

    sent = []

    def send(src, dst, sems, where):
        copy = pltpu.make_async_remote_copy(
            src_ref=src, dst_ref=dst, send_sem=sems.at[0], recv_sem=sems.at[1],
            device_id=where, device_id_type=MESH,
        )
        copy.start()
        sent.append(copy)

    def arrived(ref, sems, where):
        pltpu.make_async_remote_copy(
            src_ref=ref, dst_ref=ref, send_sem=sems.at[0], recv_sem=sems.at[1],
            device_id=where, device_id_type=MESH,
        ).wait_recv()

    to_sib = {"tok": sibling}

    z_order = [*range(1, nz), 0]
    theirs = dot(hot[0], outer[...]).astype(BF16)
    for j in range(nz):
        sib_out[j] = theirs[j * qb : (j + 1) * qb]
    pl.semaphore_wait(barrier, 1 + (nz - 1) + (nc - 1))
    for j in z_order:
        send(sib_out.at[j], sib_in.at[j], sib_sem.at[j], to_sib)
    mine = dot(hot[1], outer[...])
    for j in range(nz):
        own[j] = mine[j * qb : (j + 1) * qb]
    for j in z_order:
        arrived(sib_in.at[j], sib_sem.at[j], to_sib)
        both = own[j] + sib_in[j].astype(F32)
        if j:
            z_out[j] = both.astype(BF16)
            send(z_out.at[j], z_in.at[j], z_sem.at[j], {"tok": z_at(j)})
        else:
            own[0] = both
    total = own[0]
    for j in range(1, nz):
        arrived(z_in.at[j], z_sem.at[j], {"tok": z_at(j)})
        total = total + z_in[j].astype(F32)
    summed[...] = total.astype(BF16)

    for m in reversed(range(nc)):
        wh_loads[m].wait()
        product = dot(summed[...], wh[m])
        if m:
            c_out[m] = product.astype(BF16)
            send(c_out.at[m], c_in.at[m], c_sem.at[m], {"cell": cell_at(m)})
        else:
            own_w[...] = product
    total = own_w[...]
    for m in range(1, nc):
        arrived(c_in.at[m], c_sem.at[m], {"cell": cell_at(m)})
        total = total + c_in[m].astype(F32)
    gath[0, tok] = total.astype(BF16)

    half = qb // 2

    def order(m):
        return bin(m).count("1")

    slots = sorted(range(nc), key=order)

    def forward(s, j):
        at = z_from(j) + core
        for m in slots:
            if order(m) != order(s) + 1 or (m & s) != s:
                continue
            step = m ^ s
            where = {"cell": cell_at(step)}
            if order(m) == 1:
                send(gath.at[s, at], gath.at[m, at], gc_sem.at[m, j, 0], where)
                continue
            if step == 1 << (m.bit_length() - 1):
                part = pl.ds(0, half)
                send(gath.at[s, at, part], gath.at[m, at, part], gc_sem.at[m, j, 0], where)
            if step == m & -m:
                part = pl.ds(half, half)
                send(gath.at[s, at, part], gath.at[m, at, part], gc_sem.at[m, j, 1], where)
        send(gath.at[s, at], gath.at[s, at], gs_sem.at[s, j], to_sib)

    def take(m, j):
        at = z_from(j) + core
        if order(m) == 1:
            arrived(gath.at[m, at], gc_sem.at[m, j, 0], {"cell": cell_at(m)})
        else:
            for h, step in ((0, 1 << (m.bit_length() - 1)), (1, m & -m)):
                part = pl.ds(h * half, half)
                arrived(gath.at[m, at, part], gc_sem.at[m, j, h], {"cell": cell_at(step)})

    def multiply(m):
        for j in range(nz):
            at = z_from(j) + (1 - core)
            arrived(gath.at[m, at], gs_sem.at[m, j], to_sib)
        st_loads[m].wait()
        width = tile_of(out_ref.shape[1], 512)

        @pl.loop(0, out_ref.shape[1] // width)
        def _(n):
            cols = pl.ds(pl.multiple_of(n * width, width), width)
            piece = dot_t(gath[m].reshape(Q, fw), st[m, cols, :])
            if m == 0:
                out_ref[:, cols] = piece
            else:
                out_ref[:, cols] += piece

    for j in range(1, nz):
        send(gath.at[0, tok], gath.at[0, tok], gz_sem.at[j], {"tok": z_at(j)})
    forward(0, 0)
    ones = [m for m in slots if order(m) == 1]
    more = [m for m in slots if order(m) > 1]
    for j in range(1, nz):
        at = z_from(j) + core
        arrived(gath.at[0, at], gz_sem.at[j], {"tok": z_at(j)})
        forward(0, j)
        for m in ones:
            take(m, j - 1)
            forward(m, j - 1)
    multiply(0)
    for m in ones:
        take(m, nz - 1)
        forward(m, nz - 1)
    todo = list(ones)
    for m in more:
        for j in range(nz):
            take(m, j)
            forward(m, j)
            if todo and j >= nz // 2 - 1 and j < nz - 1:
                multiply(todo.pop(0))
        todo.append(m)
    for m in todo:
        multiply(m)
    for copy in sent:
        copy.wait_send()


def shards(nt, nc, activations, out_grads, query_ids, live, proj_in, proj_out, whitener, stores):
    toks, d = activations.shape
    kv, rb = proj_out.shape
    ra = proj_in.shape[1]
    fc, feat = whitener.shape
    fw = feat // nc
    n_stores = stores.shape[0]
    nz = nt // CORES
    qb = Q // nt
    hbm = pl.BlockSpec(memory_space=pltpu.HBM)
    vmem = pl.BlockSpec(memory_space=pltpu.VMEM)
    n_loads = 3 + 2 * (toks // tile_of(toks, 256)) + 2 * nc
    dma = pltpu.SemaphoreType.DMA
    return pl.pallas_call(
        functools.partial(kernel, nt, nc),
        out_shape=pltpu.VMEM((Q, n_stores), F32),
        in_specs=[
            hbm, hbm, hbm, pl.BlockSpec(memory_space=pltpu.SMEM),
            hbm, hbm, hbm, hbm,
        ],
        out_specs=vmem,
        scratch_shapes=[
            pltpu.VMEM((toks, d), BF16),
            pltpu.VMEM((toks, kv), BF16),
            pltpu.VMEM((1, toks), jnp.int32),
            pltpu.VMEM((ra, d), BF16),
            pltpu.VMEM((rb, kv), BF16),
            pltpu.VMEM((nc, fc, fw), BF16),
            pltpu.VMEM((nc, n_stores, fw), BF16),
            pltpu.VMEM((toks, fc), BF16),
            pltpu.VMEM((2, nz * qb, toks), BF16),
            pltpu.VMEM((nz, qb, fc), BF16),
            pltpu.VMEM((nz, qb, fc), BF16),
            pltpu.VMEM((nz, qb, fc), F32),
            pltpu.VMEM((nz, qb, fc), BF16),
            pltpu.VMEM((nz, qb, fc), BF16),
            pltpu.VMEM((qb, fc), BF16),
            pltpu.VMEM((nc, qb, fw), BF16),
            pltpu.VMEM((nc, qb, fw), BF16),
            pltpu.VMEM((qb, fw), F32),
            pltpu.VMEM((nc, nt, qb, fw), BF16),
            dma((n_loads,)),
            dma((nz, 2)),
            dma((nz, 2)),
            dma((nc, 2)),
            dma((nz, 2)),
            dma((nc, nz, 2, 2)),
            dma((nc, nz, 2)),
        ],
        compiler_params=pltpu.CompilerParams(
            collective_id=0, has_side_effects=True, vmem_limit_bytes=60 * 2**20
        ),
        cost_estimate=pl.CostEstimate(
            flops=2 * Q * n_stores * feat, bytes_accessed=24 * 2**20, transcendentals=0
        ),
        name="influence_scores",
    )(activations, out_grads, query_ids.reshape(1, toks), live, proj_in.T, proj_out.T, whitener, stores)


def solution(mesh):
    in_specs = (
        P("tok", None),
        P("tok", None),
        P("tok"),
        P("tok"),
        P(None, "cell"),
        P(),
        P("cell", None),
        P(("tok", "cell"), None),
    )
    out_specs = P(None, ("tok", "cell"))
    body = functools.partial(shards, mesh.shape["tok"], mesh.shape["cell"])
    return jax.shard_map(body, mesh=mesh, in_specs=in_specs, out_specs=out_specs, check_vma=False)
```

profile of v0, /device:TPU:0, one launch (start us, length us, event | category | flops | bytes accessed | tf_op | source)
XLA Modules:
  0.0 50.3 jit_solution(10551530543330509725)
XLA Ops:
  0.7 48.0 %influence_scores.1 = f32[512,1536]{1,0:T(8,128)S(1)} custom-call(bf16[1024,4096]{1,0:T(8,128)(2,1)} %act_hbm.1, bf16[1024,1024]{1,0:T(8,128)(2,1)} %og_hbm.1, s32[1,1024]{1,0:T(1,128)} %bitcast.5, s32[1]{0:T(128)S(6)} %copy.11.live_ref, bf16[16,4096]{1,0:T(8,128)(2,1)} %bitcast.3, bf16[32,1024]{1,0:T(8,128)(2,1)} %bitcast.4, bf16[512,2048]{1,0:T(8,128)(2,1)} %wh_hbm.1, ...), custom_call_target="tpu_custom_call" | custom-call | flops 3221225472 | bytes 25165824 | tf_op jit(solution)/shard_map/influence_scores/pallas_call | solution.py:279
  48.6 1.7 %copy.10 = f32[512,1536]{1,0:T(8,128)} copy(f32[512,1536]{1,0:T(8,128)S(1)} %influence_scores.1) | data formatting | bytes 6291456
where the time goes:
time: 50.5 us; the launch traced here: 50.3 us
  Pallas kernels  48 us (95%)
  local copies, waits for them, and re-layouts  1.67 us (3%)
  between operations  0.66 us (1%)
    pallas_call x1, Pallas kernels, shards(): pl.pallas_call(functools.partial(kernel, nt, nc), out_shape=pltpu.VMEM((Q...  48 us
    unnamed x1, local copies, waits for them, and re-layouts  1.67 us

commit v1 on v0

--- a/solution.py
+++ b/solution.py
@@ -29,10 +29,18 @@
     return lax.dot_general(a, b, (((1,), (1,)), ((), ())), preferred_element_type=F32)
 
 
-def spread(values, pattern):
-    high = values.astype(BF16)
-    low = (values - high.astype(F32)).astype(BF16)
-    return dot(high, pattern) + dot(low, pattern)
+def spread(twice, pattern):
+    high = twice.astype(BF16).astype(F32)
+    lane = lax.broadcasted_iota(jnp.int32, twice.shape, 1)
+    return dot(jnp.where(lane < twice.shape[1] // 2, high, twice - high).astype(BF16), pattern)
+
+
+def flipped(index, m):
+    other = index
+    for k in range(m.bit_length()):
+        if m & (1 << k):
+            other = other + (1 << k) * (1 - 2 * ((index // (1 << k)) % 2))
+    return other
 
 
 def kernel(
@@ -48,21 +56,13 @@
     toks, fc = outer.shape
     qb = Q // nt
     fw = wh.shape[2]
-    ra, rb = pin.shape[0], pout.shape[0]
-    bits = nc.bit_length() - 1
+    ra, rb = pin.shape[1], pout.shape[1]
 
     def cell_at(m):
-        other = cell
-        for k in range(bits):
-            if m & (1 << k):
-                other = other + (1 << k) * (1 - 2 * ((cell // (1 << k)) % 2))
-        return other
+        return flipped(cell, m)
 
     def z_at(j):
-        return ((zz + j) % nz) * CORES + core
-
-    def z_from(j):
-        return ((zz + nz - j) % nz) * CORES
+        return flipped(zz, j) * CORES + core
 
     sibling = zz * CORES + (1 - core)
 
@@ -84,8 +84,7 @@
         return copy
 
     ids_load = load(ids_hbm, ids_ref)
-    pin_load = load(pin_hbm, pin)
-    pout_load = load(pout_hbm, pout)
+    small_loads = [load(src, dst.at[n]) for src, dst in ((pin_hbm, pin), (pout_hbm, pout)) for n in range(2)]
     chunk_loads = []
     for s in range(steps):
         part = pl.ds(s * rows, rows)
@@ -103,24 +102,27 @@
     for side in range(2):
         parity = 1 - core if side == 0 else core
         for j in range(nz):
-            first = (((zz + j) % nz) * CORES + parity) * qb
+            first = (flipped(zz, j) * CORES + parity) * qb
             hot[side, pl.ds(j * qb, qb), :] = (row + first == ids).astype(F32).astype(BF16)
 
-    feat = lax.broadcasted_iota(jnp.int32, (ra, fc), 1)
-    at = lax.broadcasted_iota(jnp.int32, (ra, fc), 0)
-    left_pat = ((feat >= at * rb) & (feat < at * rb + rb)).astype(F32).astype(BF16)
-    feat = lax.broadcasted_iota(jnp.int32, (rb, fc), 1)
-    at = lax.broadcasted_iota(jnp.int32, (rb, fc), 0)
-    right_pat = (jnp.bitwise_and(feat, rb - 1) == at).astype(F32).astype(BF16)
-
-    pin_load.wait()
-    pout_load.wait()
+    def pattern(n, test):
+        feat = lax.broadcasted_iota(jnp.int32, (2 * n, fc), 1)
+        at = lax.broadcasted_iota(jnp.int32, (2 * n, fc), 0)
+        return test(feat, jnp.where(at < n, at, at - n)).astype(F32).astype(BF16)
+
+    left_pat = pattern(ra, lambda feat, at: (feat >= at * rb) & (feat < at * rb + rb))
+    right_pat = pattern(rb, lambda feat, at: jnp.bitwise_and(feat, rb - 1) == at)
+
+    for copy in small_loads:
+        copy.wait()
+    pin_twice = pin[...].reshape(2 * ra, pin.shape[2])
+    pout_twice = pout[...].reshape(2 * rb, pout.shape[2])
     for s in range(steps):
         part = pl.ds(s * rows, rows)
         chunk_loads[s][0].wait()
-        right = dot_t(og[part, :], pout[...])
+        right = dot_t(og[part, :], pout_twice)
         chunk_loads[s][1].wait()
-        left = dot_t(act[part, :], pin[...])
+        left = dot_t(act[part, :], pin_twice)
         outer[part, :] = (spread(left, left_pat) * spread(right, right_pat)).astype(BF16)
 
     for m in range(nc):
@@ -191,7 +193,7 @@
     slots = sorted(range(nc), key=order)
 
     def forward(s, j):
-        at = z_from(j) + core
+        at = z_at(j)
         for m in slots:
             if order(m) != order(s) + 1 or (m & s) != s:
                 continue
@@ -209,7 +211,7 @@
         send(gath.at[s, at], gath.at[s, at], gs_sem.at[s, j], to_sib)
 
     def take(m, j):
-        at = z_from(j) + core
+        at = z_at(j)
         if order(m) == 1:
             arrived(gath.at[m, at], gc_sem.at[m, j, 0], {"cell": cell_at(m)})
         else:
@@ -219,7 +221,7 @@
 
     def multiply(m):
         for j in range(nz):
-            at = z_from(j) + (1 - core)
+            at = z_at(j) + 1 - 2 * core
             arrived(gath.at[m, at], gs_sem.at[m, j], to_sib)
         st_loads[m].wait()
         width = tile_of(out_ref.shape[1], 512)
@@ -239,17 +241,16 @@
     ones = [m for m in slots if order(m) == 1]
     more = [m for m in slots if order(m) > 1]
     for j in range(1, nz):
-        at = z_from(j) + core
-        arrived(gath.at[0, at], gz_sem.at[j], {"tok": z_at(j)})
-        forward(0, j)
         for m in ones:
             take(m, j - 1)
             forward(m, j - 1)
-    multiply(0)
+        at = z_at(j)
+        arrived(gath.at[0, at], gz_sem.at[j], {"tok": at})
+        forward(0, j)
     for m in ones:
         take(m, nz - 1)
         forward(m, nz - 1)
-    todo = list(ones)
+    todo = [0, *ones]
     for m in more:
         for j in range(nz):
             take(m, j)
@@ -274,7 +275,7 @@
     qb = Q // nt
     hbm = pl.BlockSpec(memory_space=pltpu.HBM)
     vmem = pl.BlockSpec(memory_space=pltpu.VMEM)
-    n_loads = 3 + 2 * (toks // tile_of(toks, 256)) + 2 * nc
+    n_loads = 5 + 2 * (toks // tile_of(toks, 256)) + 2 * nc
     dma = pltpu.SemaphoreType.DMA
     return pl.pallas_call(
         functools.partial(kernel, nt, nc),
@@ -288,8 +289,8 @@
             pltpu.VMEM((toks, d), BF16),
             pltpu.VMEM((toks, kv), BF16),
             pltpu.VMEM((1, toks), jnp.int32),
-            pltpu.VMEM((ra, d), BF16),
-            pltpu.VMEM((rb, kv), BF16),
+            pltpu.VMEM((2, ra, d), BF16),
+            pltpu.VMEM((2, rb, kv), BF16),
             pltpu.VMEM((nc, fc, fw), BF16),
             pltpu.VMEM((nc, n_stores, fw), BF16),
             pltpu.VMEM((toks, fc), BF16),

time: 50.5 us -> 53.7 us (1.063)
  Pallas kernels: 48 us -> 51.2 us
    pallas_call x1, Pallas kernels: 48 us -> 51.2 us  [shards(): pl.pallas_call(functools.partial(kernel, nt, nc), out_shape=pltpu.VMEM((Q...]
where the time goes in v1:
time: 53.7 us; the launch traced here: 53.5 us
  Pallas kernels  51.2 us (95%)
  local copies, waits for them, and re-layouts  1.67 us (3%)
  between operations  0.66 us (1%)
    pallas_call x1, Pallas kernels, shards(): pl.pallas_call(functools.partial(kernel, nt, nc), out_shape=pltpu.VMEM((Q...  51.2 us
    unnamed x1, local copies, waits for them, and re-layouts  1.67 us

profile of v1, /device:TPU:0, one launch (start us, length us, event | category | flops | bytes accessed | tf_op | source)
XLA Modules:
  0.0 53.5 jit_solution(2200373843667692122)
XLA Ops:
  0.7 51.2 %influence_scores.1 = f32[512,1536]{1,0:T(8,128)S(1)} custom-call(bf16[1024,4096]{1,0:T(8,128)(2,1)} %act_hbm.1, bf16[1024,1024]{1,0:T(8,128)(2,1)} %og_hbm.1, s32[1,1024]{1,0:T(1,128)} %bitcast.5, s32[1]{0:T(128)S(6)} %copy.11.live_ref, bf16[16,4096]{1,0:T(8,128)(2,1)} %bitcast.3, bf16[32,1024]{1,0:T(8,128)(2,1)} %bitcast.4, bf16[512,2048]{1,0:T(8,128)(2,1)} %wh_hbm.1, ...), custom_call_target="tpu_custom_call" | custom-call | flops 3221225472 | bytes 25165824 | tf_op jit(solution)/shard_map/influence_scores/pallas_call | solution.py:280
  51.8 1.7 %copy.10 = f32[512,1536]{1,0:T(8,128)} copy(f32[512,1536]{1,0:T(8,128)S(1)} %influence_scores.1) | data formatting | bytes 6291456

commit v2 on v1

--- a/solution.py
+++ b/solution.py
@@ -219,47 +219,74 @@
                 part = pl.ds(h * half, half)
                 arrived(gath.at[m, at, part], gc_sem.at[m, j, h], {"cell": cell_at(step)})
 
-    def multiply(m):
-        for j in range(nz):
-            at = z_at(j) + 1 - 2 * core
-            arrived(gath.at[m, at], gs_sem.at[m, j], to_sib)
-        st_loads[m].wait()
-        width = tile_of(out_ref.shape[1], 512)
-
-        @pl.loop(0, out_ref.shape[1] // width)
-        def _(n):
-            cols = pl.ds(pl.multiple_of(n * width, width), width)
-            piece = dot_t(gath[m].reshape(Q, fw), st[m, cols, :])
-            if m == 0:
-                out_ref[:, cols] = piece
-            else:
-                out_ref[:, cols] += piece
+    width = tile_of(out_ref.shape[1], 512)
+    side_rows = nt // 2
+
+    def multiply(parts, far, cols):
+        top = zz // (nz // 2)
+        first = ((1 - top) if far else top) * side_rows
+        lhs = [gath[m, pl.ds(first, side_rows)].reshape(side_rows * qb, fw) for m in parts]
+        rhs = [st[m, cols, :] for m in parts]
+        piece = dot_t(jnp.concatenate(lhs, axis=1), jnp.concatenate(rhs, axis=1))
+        out_ref[pl.ds(pl.multiple_of(first * qb, 128), side_rows * qb), cols] = piece
+
+    def from_sibling(m, j):
+        arrived(gath.at[m, z_at(j) + 1 - 2 * core], gs_sem.at[m, j], to_sib)
+
+    ones = [m for m in slots if order(m) == 1]
+    more = [m for m in slots if order(m) > 1]
+    base = [0, *ones]
+    tiles = out_ref.shape[1] // width
+    units = [(far, n) for far in range(2) for n in range(tiles)]
+
+    def run(count):
+        for far, n in units[:count]:
+            if n == 0:
+                for m in base:
+                    if not far:
+                        st_loads[m].wait()
+                    for j in range(far * (nz // 2), (far + 1) * (nz // 2)):
+                        from_sibling(m, j)
+            multiply(base, far, pl.ds(n * width, width))
+        del units[:count]
 
     for j in range(1, nz):
         send(gath.at[0, tok], gath.at[0, tok], gz_sem.at[j], {"tok": z_at(j)})
     forward(0, 0)
-    ones = [m for m in slots if order(m) == 1]
-    more = [m for m in slots if order(m) > 1]
+    def pass_on(group, j):
+        for m in group:
+            take(m, j)
+            forward(m, j)
+
+    taken = 0
     for j in range(1, nz):
-        for m in ones:
-            take(m, j - 1)
-            forward(m, j - 1)
+        pass_on(ones, j - 1)
+        if j > nz // 2:
+            pass_on(more, taken)
+            taken += 1
         at = z_at(j)
         arrived(gath.at[0, at], gz_sem.at[j], {"tok": at})
         forward(0, j)
-    for m in ones:
-        take(m, nz - 1)
-        forward(m, nz - 1)
-    todo = [0, *ones]
+        if j >= nz // 2:
+            run(1)
+    pass_on(ones, nz - 1)
+    while taken < nz:
+        pass_on(more, taken)
+        taken += 1
+        if taken < nz:
+            run(1)
+    run(len(units))
     for m in more:
+        st_loads[m].wait()
         for j in range(nz):
-            take(m, j)
-            forward(m, j)
-            if todo and j >= nz // 2 - 1 and j < nz - 1:
-                multiply(todo.pop(0))
-        todo.append(m)
-    for m in todo:
-        multiply(m)
+            from_sibling(m, j)
+
+    @pl.loop(0, tiles)
+    def _(n):
+        cols = pl.ds(pl.multiple_of(n * width, width), width)
+        for m in more:
+            out_ref[:, cols] += dot_t(gath[m].reshape(Q, fw), st[m, cols, :])
+
     for copy in sent:
         copy.wait_send()
 

time: 53.7 us -> 51.5 us (0.959)
  Pallas kernels: 51.2 us -> 49 us
    pallas_call x1, Pallas kernels: 51.2 us -> 49 us  [shards(): pl.pallas_call(functools.partial(kernel, nt, nc), out_shape=pltpu.VMEM((Q...]
where the time goes in v2:
time: 51.5 us; the launch traced here: 51.3 us
  Pallas kernels  49 us (95%)
  local copies, waits for them, and re-layouts  1.67 us (3%)
  between operations  0.66 us (1%)
    pallas_call x1, Pallas kernels, shards(): pl.pallas_call(functools.partial(kernel, nt, nc), out_shape=pltpu.VMEM((Q...  49 us
    unnamed x1, local copies, waits for them, and re-layouts  1.67 us

profile of v2, /device:TPU:0, one launch (start us, length us, event | category | flops | bytes accessed | tf_op | source)
XLA Modules:
  0.0 51.3 jit_solution(10646561252011405368)
XLA Ops:
  0.7 49.0 %influence_scores.1 = f32[512,1536]{1,0:T(8,128)S(1)} custom-call(bf16[1024,4096]{1,0:T(8,128)(2,1)} %act_hbm.1, bf16[1024,1024]{1,0:T(8,128)(2,1)} %og_hbm.1, s32[1,1024]{1,0:T(1,128)} %bitcast.5, s32[1]{0:T(128)S(6)} %copy.11.live_ref, bf16[16,4096]{1,0:T(8,128)(2,1)} %bitcast.3, bf16[32,1024]{1,0:T(8,128)(2,1)} %bitcast.4, bf16[512,2048]{1,0:T(8,128)(2,1)} %wh_hbm.1, ...), custom_call_target="tpu_custom_call" | custom-call | flops 3221225472 | bytes 25165824 | tf_op jit(solution)/shard_map/influence_scores/pallas_call | solution.py:307
  49.6 1.7 %copy.10 = f32[512,1536]{1,0:T(8,128)} copy(f32[512,1536]{1,0:T(8,128)S(1)} %influence_scores.1) | data formatting | bytes 6291456
